TPU v7x, 32 devices: a whole 2x2x4 slice. The times are simulated.
32 devices in a mesh: gx: 4 (over y, core), gy: 8 (over z, x).
Axes of the slice: x: 2, y: 2, z: 4, core: 2. Of those that a mesh axis runs over, the one named last changes fastest.
Arguments:
- dens_pres: float32 [2, 32, 128, 128], P(None, 'gx', 'gy'), may hold values from 0.7 to 1.3
- velocity: float32 [3, 32, 128, 128], P(None, 'gx', 'gy'), may hold values from -0.9 to 0.9
- cut_class: int32 [32, 128, 128], P('gx', 'gy'), may hold values from 0 to 3
- nbhd_cells: int32 [4, 8, 32, 64], P('gx', 'gy'), may hold values from 0 to 16383, as said below
- helper_list: int32 [4, 8, 32], P('gx', 'gy'), may hold values from 0 to 7, as said below
- live_counts: int32 [4, 8], P('gx', 'gy'), may hold values from 16 to 32, as said below
- redist_weights: float32 [4, 8, 8, 8, 64, 64], P('gx', 'gy'), may hold values from -0.2 to 0.7
Outputs:
- new_state: float32 [5, 32, 128, 128], P(None, 'gx', 'gy')
Inputs may be any that keep to these rules, and one draw needn't show every extreme that they name: `nbhd_cells`: in each grid block the 32 x 64 entries are distinct cell numbers of that block. `helper_list`: in each grid block no helper is named by more than 8 slots, and at least one helper is named by exactly 8. `live_counts`: the slots below the count are live.
All inputs are finite; a program needn't handle non-finite values.
Results may differ from a plain program's by a relative error of at most 0.0003.
Values sent between devices are 32-bit elements; how exact they have to be, the bound alone decides.
A program may use at most 64 MiB of HBM per device.

v0:
```python
import jax
import jax.numpy as jnp
from jax import lax
from jax.sharding import PartitionSpec as P

GAS_GAMMA = 1.4
STEP_RATIO = 0.3


def padded_2(cells, sides, width):
    for axis, dim in sides:
        count = lax.axis_size(axis)
        head = lax.slice_in_dim(cells, 0, width, axis=dim)
        tail = lax.slice_in_dim(cells, cells.shape[dim] - width, cells.shape[dim], axis=dim)
        cells = jnp.concatenate(
            [
                lax.ppermute(tail, axis, [(i, (i + 1) % count) for i in range(count)]),
                cells,
                lax.ppermute(head, axis, [((i + 1) % count, i) for i in range(count)]),
            ],
            axis=dim,
        )
    return cells


def minmod(lower_diff, upper_diff):
    return (
        0.5
        * (jnp.sign(lower_diff) + jnp.sign(upper_diff))
        * jnp.minimum(jnp.abs(lower_diff), jnp.abs(upper_diff))
    )


def conserved(primitive):
    density = primitive[0]
    speeds = primitive[1:4]
    pressure = primitive[4]
    energy = pressure / (GAS_GAMMA - 1.0) + 0.5 * density * jnp.sum(speeds * speeds, axis=0)
    return jnp.concatenate([density[None], density[None] * speeds, energy[None]], axis=0)


def face_flux(primitive, normal):
    density = primitive[0]
    pressure = primitive[4]
    normal_speed = primitive[1 + normal]
    state = conserved(primitive)
    flux = state * normal_speed[None]
    flux = flux.at[1 + normal].add(pressure)
    flux = flux.at[4].add(pressure * normal_speed)
    sound = jnp.sqrt(GAS_GAMMA * pressure / density)
    return (state, flux, jnp.abs(normal_speed) + sound)


def rusanov(lower_state, upper_state, normal):
    cons_low, flux_low, speed_low = face_flux(lower_state, normal)
    cons_up, flux_up, speed_up = face_flux(upper_state, normal)
    wave = jnp.maximum(speed_low, speed_up)
    return 0.5 * (flux_low + flux_up) - 0.5 * wave[None] * (cons_up - cons_low)


def piece(array, start, stop, axis):
    return lax.slice_in_dim(array, start, stop, axis=axis)


def divergence(padded, normal):
    axis = normal + 1
    length = padded.shape[axis] - 4
    jumps = piece(padded, 1, length + 4, axis) - piece(padded, 0, length + 3, axis)
    slopes = minmod(piece(jumps, 0, length + 2, axis), piece(jumps, 1, length + 3, axis))
    centres = piece(padded, 1, length + 3, axis)
    lower_state = piece(centres, 0, length + 1, axis) + 0.5 * piece(slopes, 0, length + 1, axis)
    upper_state = piece(centres, 1, length + 2, axis) - 0.5 * piece(slopes, 1, length + 2, axis)
    fluxes = rusanov(lower_state, upper_state, normal)
    return piece(fluxes, 1, length + 1, axis) - piece(fluxes, 0, length, axis)


def local(dens_pres, velocity, cut_class, nbhd_cells, helper_list, live_counts, redist_weights):
    primitive = jnp.concatenate([dens_pres[0:1], velocity, dens_pres[1:2]], axis=0)
    x_padded = padded_2(primitive, (("gx", 1),), 2)
    y_padded = padded_2(primitive, (("gy", 2),), 2)
    z_padded = jnp.pad(primitive, ((0, 0), (0, 0), (0, 0), (2, 2)), mode="wrap")
    total_div = divergence(x_padded, 0) + divergence(y_padded, 1) + divergence(z_padded, 2)
    kappa = 0.25 * (1.0 + cut_class.astype(jnp.float32))
    delta = -STEP_RATIO * total_div / kappa[None]
    flat_delta = delta.reshape(5, -1)
    total_cells = flat_delta.shape[1]
    cells = nbhd_cells[0, 0]
    helpers = helper_list[0, 0]
    slots = helpers.shape[0]
    width = cells.shape[1]
    columns = lax.axis_size("gy")
    capacity = redist_weights.shape[3]
    same = helpers[None, :] == helpers[:, None]
    lower = lax.broadcasted_iota(jnp.int32, (slots, slots), 1) < lax.broadcasted_iota(
        jnp.int32, (slots, slots), 0
    )
    ranks = jnp.sum((same & lower).astype(jnp.int32), axis=1)
    position = helpers * capacity + ranks
    placing = (
        jnp.arange(columns * capacity, dtype=jnp.int32)[:, None] == position[None, :]
    ).astype(jnp.float32)
    values = flat_delta[:, cells]
    outgoing = jnp.einsum("ps,vsw->pvw", placing, values, precision=lax.Precision.HIGHEST)
    outgoing = outgoing.reshape(columns, capacity, 5, width)
    arrived = lax.all_to_all(outgoing, "gy", split_axis=0, concat_axis=0, tiled=True)
    mixed = jnp.einsum(
        "scij,scvj->scvi", redist_weights[0, 0], arrived, precision=lax.Precision.HIGHEST
    )
    returned = lax.all_to_all(mixed, "gy", split_axis=0, concat_axis=0, tiled=True)
    results = jnp.einsum(
        "ps,pvw->vsw",
        placing,
        returned.reshape(columns * capacity, 5, width),
        precision=lax.Precision.HIGHEST,
    )
    live = jnp.arange(slots, dtype=jnp.int32) < live_counts[0, 0]
    results = jnp.where(live[None, :, None], results, values).reshape(5, slots * width)
    entry_of = (
        jnp.full((total_cells,), -1, jnp.int32)
        .at[cells.reshape(-1)]
        .set(jnp.arange(slots * width, dtype=jnp.int32))
    )
    covered = entry_of >= 0
    fetched = jnp.take(results, jnp.maximum(entry_of, 0), axis=1)
    flat_delta = jnp.where(covered[None, :], fetched, flat_delta)
    return conserved(primitive) + flat_delta.reshape(delta.shape)


def solution(mesh):
    in_specs = (
        P(None, "gx", "gy", None),
        P(None, "gx", "gy", None),
        P("gx", "gy", None),
        P("gx", "gy", None, None),
        P("gx", "gy", None),
        P("gx", "gy"),
        P("gx", "gy", None, None, None, None),
    )
    out_specs = P(None, "gx", "gy", None)
    return jax.shard_map(local, mesh=mesh, in_specs=in_specs, out_specs=out_specs, check_vma=False)
```

profile of v0, /device:TPU:0, one launch (start us, length us, event | category | flops | bytes accessed | tf_op | source)
XLA Modules:
  0.0 148.0 jit_solution(10878904666307908515)
XLA Ops:
  0.0 1.7 %fusion.56 = (f32[1,8,16,128]{3,2,1,0:T(8,128)S(1)}, f32[8,16,128]{2,1,0:T(8,128)}, f32[1,8,16,128]{3,2,1,0:T(8,128)S(1)}) fusion(f32[2,8,16,128]{3,2,1,0:T(8,128)} %param.31), kind=kLoop, calls=%fused_computation.167 | loop fusion | bytes 327680 | tf_op jit(solution)/shard_map/slice | solution.py:78
  1.7 0.9 fusion.15
  3.8 2.0 %collective-permute-start.1 = (f32[5,2,16,128]{3,2,1,0:T(8,128)}, f32[5,2,16,128]{3,2,1,0:T(8,128)}, u32[]{:S(2)}, u32[]{:S(2)}) collective-permute-start(f32[5,2,16,128]{3,2,1,0:T(8,128)} %get-tuple-element.183), channel_id=1, source_target_pairs={{8,0},{16,8},{24,16},{0,24},{9,1},{17,9},{25,17},{1,25},{10,2},{18... | collective-permute-start | bytes 245768 | tf_op jit(solution)/shard_map/ppermute | solution.py:19
  6.4 2.3 %collective-permute-start.2 = (f32[5,8,2,128]{3,2,1,0:T(2,128)}, f32[5,8,2,128]{3,2,1,0:T(2,128)}, u32[]{:S(2)}, u32[]{:S(2)}) collective-permute-start(f32[5,8,2,128]{3,2,1,0:T(2,128)} %get-tuple-element.184), channel_id=1, source_target_pairs={{0,1},{1,2},{2,3},{3,4},{4,5},{5,6},{6,7},{7,0},{8,9},{9,10},{10,1... | collective-permute-start | bytes 122888 | tf_op jit(solution)/shard_map/ppermute | solution.py:17
  8.7 3.0 %collective-permute-start.3 = (f32[5,8,2,128]{3,2,1,0:T(2,128)}, f32[5,8,2,128]{3,2,1,0:T(2,128)}, u32[]{:S(2)}, u32[]{:S(2)}) collective-permute-start(f32[5,8,2,128]{3,2,1,0:T(2,128)} %get-tuple-element.185), channel_id=1, source_target_pairs={{1,0},{2,1},{3,2},{4,3},{5,4},{6,5},{7,6},{0,7},{9,8},{10,9},{11,1... | collective-permute-start | bytes 122888 | tf_op jit(solution)/shard_map/ppermute | solution.py:19
  11.9 1.3 compare_select_fusion.1
  14.0 8.1 %scatter_custom_fusion = s32[16384]{0:T(1024)S(1)} fusion(s32[2048]{0:T(1024)S(1)} %bitcast.119, s32[2048]{0:T(1024)S(1)} %iota.22, s32[]{:T(128)} %constant.324.clone.1), kind=kCustom, calls=%fused_computation.145 | custom fusion | bytes 65540 | tf_op jit(solution)/shard_map/scatter | solution.py:121
  23.4 1.2 pad_maximum_fusion.6
  29.3 1.4 reshape.504
  30.7 1.3 broadcast_clamp_fusion
  32.0 0.9 convert_reduce_fusion
  32.9 1.7 %multiply_subtract_fusion = f32[5,8,16,129]{3,2,1,0:T(8,128)S(1)} fusion(f32[5,8,16,129]{3,2,1,0:T(8,128)} %copy-done.2, f32[5,8,16,129]{3,2,1,0:T(8,128)S(1)} %fusion.25, f32[1,8,16,129]{3,2,1,0:T(8,128)} %copy-done.8, f32[3,8,16,129]{3,2,1,0:T(8,128)S(1)} %slice_multiply_fusion.4, f32[1,8,16,129]{3,2,1,0:T(8,128)} %copy-done.9, ...), kind=kLoop, calls=%fused_computation.22 | loop fusion | flops 743040 | bytes 1717248 | tf_op jit(solution)/shard_map/sub | solution.py:58
  36.6 1.0 fusion.5
  38.2 0.9 pad_maximum_fusion.15
  41.0 4.7 %copy.22 = f32[5,8,16,128]{0,3,2,1:T(8,128)} copy(f32[5,8,16,128]{3,2,1,0:T(8,128)S(1)} %fusion.18) | data formatting | bytes 655360 | tf_op jit(solution)/shard_map/div | solution.py:84
  45.7 10.9 %gather_fusion = f32[2048,5]{1,0:T(8,128)} fusion(f32[5,16384]{0,1:T(8,128)} %bitcast.111, s32[2048]{0:T(1024)S(1)} %copy-done.16), kind=kCustom, calls=%fused_computation | custom fusion | bytes 90112 | tf_op jit(solution)/shard_map/gather | solution.py:102
  56.7 1.6 %copy.30 = f32[32,64,5]{1,0,2:T(8,128)S(1)} copy(f32[32,64,5]{2,1,0:T(8,128)} %bitcast.113) | data formatting | bytes 81920 | tf_op jit(solution)/shard_map/gather | solution.py:102
  59.4 3.4 %all-to-all-start = ((f32[8,1,2560]{2,1,0:T(1,128)}), f32[8,1,2560]{2,1,0:T(1,128)S(1)}, u32[]{:S(2)}, u32[]{:S(2)}) async-start(f32[8,1,2560]{2,1,0:T(1,128)} %reshape.531), calls=%async_computation | async-start | bytes 163840 | tf_op jit(solution)/shard_map/all_to_all | solution.py:105
  63.5 6.2 %all-to-all-done = f32[8,1,2560]{2,1,0:T(1,128)S(1)} async-done(((f32[8,1,2560]{2,1,0:T(1,128)}), f32[8,1,2560]{2,1,0:T(1,128)S(1)}, u32[]{:S(2)}, u32[]{:S(2)}) %all-to-all-start) | async-done | bytes 81952 | tf_op jit(solution)/shard_map/all_to_all | solution.py:105
  71.3 3.4 %fusion = f32[8,8,5,64]{3,2,1,0:T(8,128)S(1)} fusion(f32[1,1,8,8,64,64]{5,4,3,2,1,0:T(8,128)S(1)} %copy-done, f32[8,8,5,64]{3,1,2,0:T(8,128)S(1)} %bitcast.114), kind=kOutput, calls=%fused_computation.3 | convolution fusion | flops 15728640 | bytes 1212416 | tf_op jit(solution)/shard_map/scij,scvj->scvi/dot_general | solution.py:106
  75.5 3.4 %all-to-all-start.1 = ((f32[8,1,2560]{2,1,0:T(1,128)}), f32[8,1,2560]{2,1,0:T(1,128)S(1)}, u32[]{:S(2)}, u32[]{:S(2)}) async-start(f32[8,1,2560]{2,1,0:T(1,128)} %reshape.533), calls=%async_computation.1 | async-start | bytes 163840 | tf_op jit(solution)/shard_map/all_to_all | solution.py:109
  80.2 5.6 %all-to-all-done.1 = f32[8,1,2560]{2,1,0:T(1,128)S(1)} async-done(((f32[8,1,2560]{2,1,0:T(1,128)}), f32[8,1,2560]{2,1,0:T(1,128)S(1)}, u32[]{:S(2)}, u32[]{:S(2)}) %all-to-all-start.1) | async-done | bytes 81952 | tf_op jit(solution)/shard_map/all_to_all | solution.py:109
  87.5 54.4 %gather_fusion.1 = f32[16384,5]{1,0:T(8,128)} fusion(f32[5,2048]{0,1:T(8,128)S(1)} %bitcast.110, s32[16384]{0:T(1024)S(1)} %copy-done.12), kind=kCustom, calls=%fused_computation.1 | custom fusion | bytes 720896 | tf_op jit(solution)/shard_map/jit(_take)/gather | solution.py:124
  141.9 5.3 %copy.29 = f32[5,8,16,128]{3,2,1,0:T(8,128)S(1)} copy(f32[5,8,16,128]{0,3,2,1:T(8,128)} %bitcast.112) | data formatting | bytes 655360 | tf_op jit(solution)/shard_map/jit(_take)/gather | solution.py:124
  (113 shorter events, 20.2 us)
Async XLA Ops:
  0.0 71.3 %copy-start = (f32[1,1,8,8,64,64]{5,4,3,2,1,0:T(8,128)S(1)}, f32[1,1,8,8,64,64]{5,4,3,2,1,0:T(8,128)}, u32[]{:S(2)}) copy-start(f32[1,1,8,8,64,64]{5,4,3,2,1,0:T(8,128)} %param.37) | copy-start | bytes 3145732
  0.0 25.3 %copy-start.1 = (f32[3,8,16,128]{3,2,1,0:T(8,128)S(1)}, f32[3,8,16,128]{3,2,1,0:T(8,128)}, u32[]{:S(2)}) copy-start(f32[3,8,16,128]{3,2,1,0:T(8,128)} %param.32) | copy-start | bytes 589828
  3.3 34.9 %collective-permute-start = (f32[5,2,16,128]{3,2,1,0:T(8,128)}, f32[5,2,16,128]{3,2,1,0:T(8,128)S(1)}, u32[]{:S(2)}, u32[]{:S(2)}) collective-permute-start(f32[5,2,16,128]{3,2,1,0:T(8,128)} %get-tuple-element.182), channel_id=1, source_target_pairs={{0,8},{8,16},{16,24},{24,0},{1,9},{9,17},{17,25},{25,1},{2,10},{10... | collective-permute-start | bytes 245768 | tf_op jit(solution)/shard_map/ppermute | solution.py:17
  3.8 34.5 %collective-permute-start.1 = (f32[5,2,16,128]{3,2,1,0:T(8,128)}, f32[5,2,16,128]{3,2,1,0:T(8,128)}, u32[]{:S(2)}, u32[]{:S(2)}) collective-permute-start(f32[5,2,16,128]{3,2,1,0:T(8,128)} %get-tuple-element.183), channel_id=1, source_target_pairs={{8,0},{16,8},{24,16},{0,24},{9,1},{17,9},{25,17},{1,25},{10,2},{18... | collective-permute-start | bytes 245768 | tf_op jit(solution)/shard_map/ppermute | solution.py:19
  6.4 28.9 %collective-permute-start.2 = (f32[5,8,2,128]{3,2,1,0:T(2,128)}, f32[5,8,2,128]{3,2,1,0:T(2,128)}, u32[]{:S(2)}, u32[]{:S(2)}) collective-permute-start(f32[5,8,2,128]{3,2,1,0:T(2,128)} %get-tuple-element.184), channel_id=1, source_target_pairs={{0,1},{1,2},{2,3},{3,4},{4,5},{5,6},{6,7},{7,0},{8,9},{9,10},{10,1... | collective-permute-start | bytes 122888 | tf_op jit(solution)/shard_map/ppermute | solution.py:17
  8.7 26.7 %collective-permute-start.3 = (f32[5,8,2,128]{3,2,1,0:T(2,128)}, f32[5,8,2,128]{3,2,1,0:T(2,128)}, u32[]{:S(2)}, u32[]{:S(2)}) collective-permute-start(f32[5,8,2,128]{3,2,1,0:T(2,128)} %get-tuple-element.185), channel_id=1, source_target_pairs={{1,0},{2,1},{3,2},{4,3},{5,4},{6,5},{7,6},{0,7},{9,8},{10,9},{11,1... | collective-permute-start | bytes 122888 | tf_op jit(solution)/shard_map/ppermute | solution.py:19
  24.6 4.1 %copy-start.19 = (s32[8,16,128]{2,1,0:T(8,128)S(1)}, s32[8,16,128]{2,1,0:T(8,128)}, u32[]{:S(2)}) copy-start(s32[8,16,128]{2,1,0:T(8,128)} %param.33) | copy-start | bytes 196612
  26.8 0.9 copy-start.6
  26.8 0.9 copy-start.7
  27.1 0.7 copy-start.3
  27.9 0.8 copy-start.2
  38.0 2.8 %copy-start.13 = (f32[8,16,128]{2,1,0:T(8,128)S(1)}, f32[8,16,128]{2,1,0:T(8,128)}, u32[]{:S(2)}) copy-start(f32[8,16,128]{2,1,0:T(8,128)} %add_multiply_fusion) | copy-start | bytes 196612
  40.4 5.3 %copy-start.16 = (s32[2048]{0:T(1024)S(1)}, s32[2048]{0:T(1024)}, u32[]{:S(2)}) copy-start(s32[2048]{0:T(1024)} %broadcast_clamp_fusion) | copy-start | bytes 24580
  40.6 22.2 %copy-start.14 = (f32[8,16,128]{2,1,0:T(8,128)S(1)}, f32[8,16,128]{2,1,0:T(8,128)}, u32[]{:S(2)}) copy-start(f32[8,16,128]{2,1,0:T(8,128)} %get-tuple-element.191) | copy-start | bytes 196612
  41.0 45.8 %copy-start.4 = (f32[5,8,16,128]{3,2,1,0:T(8,128)}, f32[5,8,16,128]{3,2,1,0:T(8,128)S(1)}, u32[]{:S(2)}) copy-start(f32[5,8,16,128]{3,2,1,0:T(8,128)S(1)} %fusion.18) | copy-start | bytes 983044
  41.0 37.9 %copy-start.11 = (f32[2,8,16,128]{3,2,1,0:T(8,128)S(1)}, f32[2,8,16,128]{3,2,1,0:T(8,128)}, u32[]{:S(2)}) copy-start(f32[2,8,16,128]{3,2,1,0:T(8,128)} %param.31) | copy-start | bytes 393220
  41.0 46.4 %copy-start.12 = (s32[16384]{0:T(1024)S(1)}, s32[16384]{0:T(1024)}, u32[]{:S(2)}) copy-start(s32[16384]{0:T(1024)} %maximum_clamp_fusion) | copy-start | bytes 196612
  59.4 10.3 %all-to-all-start = ((f32[8,1,2560]{2,1,0:T(1,128)}), f32[8,1,2560]{2,1,0:T(1,128)S(1)}, u32[]{:S(2)}, u32[]{:S(2)}) async-start(f32[8,1,2560]{2,1,0:T(1,128)} %reshape.531), calls=%async_computation | async-start | bytes 163840 | tf_op jit(solution)/shard_map/all_to_all | solution.py:105
  74.7 72.5 %copy-start.10 = (f32[3,8,16,128]{3,2,1,0:T(8,128)S(1)}, f32[3,8,16,128]{3,2,1,0:T(8,128)}, u32[]{:S(2)}) copy-start(f32[3,8,16,128]{3,2,1,0:T(8,128)} %get-tuple-element.188) | copy-start | bytes 589828
  75.5 10.3 %all-to-all-start.1 = ((f32[8,1,2560]{2,1,0:T(1,128)}), f32[8,1,2560]{2,1,0:T(1,128)S(1)}, u32[]{:S(2)}, u32[]{:S(2)}) async-start(f32[8,1,2560]{2,1,0:T(1,128)} %reshape.533), calls=%async_computation.1 | async-start | bytes 163840 | tf_op jit(solution)/shard_map/all_to_all | solution.py:109
  87.4 59.8 %copy-start.15 = (f32[1,8,16,128]{3,2,1,0:T(8,128)S(1)}, f32[1,8,16,128]{3,2,1,0:T(8,128)}, u32[]{:S(2)}) copy-start(f32[1,8,16,128]{3,2,1,0:T(8,128)} %fusion.44) | copy-start | bytes 196612
  87.5 59.8 %copy-start.17 = (pred[16384]{0:T(1024)(128)(4,1)S(1)}, pred[16384]{0:T(1024)(128)(4,1)}, u32[]{:S(2)}) copy-start(pred[16384]{0:T(1024)(128)(4,1)} %get-tuple-element.193) | copy-start | bytes 49156
  141.9 5.3 %copy-start.5 = (f32[5,8,16,128]{3,2,1,0:T(8,128)S(1)}, f32[5,8,16,128]{3,2,1,0:T(8,128)}, u32[]{:S(2)}) copy-start(f32[5,8,16,128]{3,2,1,0:T(8,128)} %copy-done.4) | copy-start | bytes 983044
  141.9 5.3 %copy-start.18 = (pred[16384]{0:T(1024)(128)(4,1)S(1)}, pred[16384]{0:T(1024)(128)(4,1)}, u32[]{:S(2)}) copy-start(pred[16384]{0:T(1024)(128)(4,1)} %get-tuple-element.194) | copy-start | bytes 49156
  (2 other events, 1.3 us)
where the time goes:
time: 149 us; the launch traced here: 148 us
  local copies, waits for them, and re-layouts  94.6 us (63%)
  other arithmetic  21.9 us (15%)
  starting transfers between devices  14.4 us (10%)
  waiting for transfers between devices  11.9 us (8%)
  matrix products  3.94 us (3%)
    gather x2, local copies, waits for them, and re-layouts, local(): fetched = jnp.take(results, jnp.maximum(entry_of, 0), axis=1)  59.7 us
    gather x2, local copies, waits for them, and re-layouts, local(): values = flat_delta[:, cells]  12.5 us
    scatter x1, local copies, waits for them, and re-layouts, local(): entry_of = jnp.full((total_cells,), -1, jnp.int32).at[cells.reshape(-1)]....  8.09 us
    all_to_all x1, waiting for transfers between devices, local(): lax.all_to_all(outgoing, 'gy', split_axis=0, concat_axis=0, tiled=True)  6.23 us
    all_to_all x1, waiting for transfers between devices, local(): lax.all_to_all(mixed, 'gy', split_axis=0, concat_axis=0, tiled=True)  5.65 us
    ppermute x2, starting transfers between devices, padded_2(): lax.ppermute(head, axis, [((i + 1) % count, i) for i in range(count)])  5 us
    div x1, local copies, waits for them, and re-layouts, local(): delta = -STEP_RATIO * total_div / kappa[None]  4.7 us
    dot_general x1, matrix products, local(): jnp.einsum('scij,scvj->scvi', redist_weights[0, 0], arrived, precision=la...  3.36 us
  transfers between devices with their start and end apart: 6, of which 2 were waited for; matrix products, arithmetic and copies ran while one was open for 18% of the time, Pallas kernels for 0%

commit v1 on v0

v1 whole, which is shorter than its diff:
```python
import functools

import jax
import jax.numpy as jnp
from jax import lax
from jax.experimental import pallas as pl
from jax.experimental.pallas import tpu as pltpu
from jax.sharding import PartitionSpec as P

GAS_GAMMA = 1.4
STEP_RATIO = 0.3
MESH = pl.DeviceIdType.MESH
NT = (((1,), (1,)), ((), ()))
LANES = 128


def minmod(a, b):
    return jnp.maximum(jnp.minimum(a, b), 0.0) + jnp.minimum(jnp.maximum(a, b), 0.0)


def conserved(q):
    rho, u, v, w, p = q
    energy = p * (1.0 / (GAS_GAMMA - 1.0)) + 0.5 * rho * (u * u + v * v + w * w)
    return [rho, rho * u, rho * v, rho * w, energy]


def state_flux(q, normal):
    rho, p, un = q[0], q[4], q[1 + normal]
    cons = conserved(q)
    flux = [part * un for part in cons]
    flux[1 + normal] = flux[1 + normal] + p
    flux[4] = flux[4] + p * un
    gp = GAS_GAMMA * p
    return cons, flux, jnp.abs(un) + gp * lax.rsqrt(gp * rho)


def double_flux(lower, upper, normal):
    cl, fl, sl = state_flux(lower, normal)
    cu, fu, su = state_flux(upper, normal)
    wave = jnp.maximum(sl, su)
    return [a + b - wave * (d - c) for a, b, c, d in zip(fl, fu, cl, cu)]


def cyclic_divergence(q, normal, axis):
    size = q[0].shape[axis]
    before = lambda t: pltpu.roll(t, 1, axis)
    after = lambda t: pltpu.roll(t, size - 1, axis)
    jumps = [t - before(t) for t in q]
    halves = [0.5 * minmod(j, after(j)) for j in jumps]
    lower = [t + s for t, s in zip(q, halves)]
    upper = [after(t - s) for t, s in zip(q, halves)]
    flux = double_flux(lower, upper, normal)
    return [f - before(f) for f in flux]


def split2(t):
    high = t.astype(jnp.bfloat16)
    return high, (t - high.astype(jnp.float32)).astype(jnp.bfloat16)


def kernel(ngx, ngy, dp_ref, vel_ref, cut_ref, cells_ref, help_ref, live_ref, w_ref, out_ref,
           px, py, ysend, yrecv, cutv, wv, acc, dmat, ridx, zidx, ohr, ohz, wbd,
           sendv, arrived, mixed, returned,
           lsem, hsend, hrecv, asend, arecv, bsend, brecv):
    gx = lax.axis_index("gx")
    gy = lax.axis_index("gy")
    _, cx, cy, nz = dp_ref.shape
    cap, nbr = w_ref.shape[3], w_ref.shape[4]
    slots = cells_ref.shape[2]
    pack = LANES // nbr
    rows = cap // pack
    entries = cap * nbr
    cells_xy = cx * cy

    loads = [
        pltpu.make_async_copy(dp_ref.at[0], px.at[0, pl.ds(2, cx)], lsem.at[0]),
        pltpu.make_async_copy(dp_ref.at[1], px.at[4, pl.ds(2, cx)], lsem.at[1]),
        pltpu.make_async_copy(vel_ref, px.at[pl.ds(1, 3), pl.ds(2, cx)], lsem.at[2]),
    ]
    later = [
        pltpu.make_async_copy(w_ref.at[0, 0], wv, lsem.at[3]),
        pltpu.make_async_copy(cut_ref, cutv, lsem.at[4]),
    ]
    for copy in loads + later:
        copy.start()

    xlo = {"gx": lax.rem(gx + ngx - 1, ngx)}
    xhi = {"gx": lax.rem(gx + 1, ngx)}
    ylo = {"gy": lax.rem(gy + ngy - 1, ngy)}
    yhi = {"gy": lax.rem(gy + 1, ngy)}
    barrier = pltpu.get_barrier_semaphore()
    for target in (xlo, xhi):
        pl.semaphore_signal(barrier, inc=1, device_id=target, device_id_type=MESH)
    for k in range(1, ngy):
        pl.semaphore_signal(barrier, inc=1, device_id={"gy": lax.rem(gy + k, ngy)}, device_id_type=MESH)

    for copy in loads:
        copy.wait()

    def fill_rows(x, carry):
        for v in range(5):
            q = px[v, x + 2]
            py[v, x, pl.ds(0, cy), :] = q
            ysend[0, v, x] = q[0:2]
            ysend[1, v, x] = q[cy - 2:cy]
        return carry

    lax.fori_loop(0, cx, fill_rows, 0)
    pl.semaphore_wait(barrier, ngy + 1)

    def remote(src, dst, send, recv, target):
        return pltpu.make_async_remote_copy(src_ref=src, dst_ref=dst, send_sem=send, recv_sem=recv,
                                            device_id=target, device_id_type=MESH)

    halos = [
        remote(px.at[:, pl.ds(2, 2)], px.at[:, pl.ds(cx + 2, 2)], hsend.at[0], hrecv.at[0], xlo),
        remote(px.at[:, pl.ds(cx, 2)], px.at[:, pl.ds(0, 2)], hsend.at[1], hrecv.at[1], xhi),
        remote(ysend.at[0], yrecv.at[1], hsend.at[2], hrecv.at[2], ylo),
        remote(ysend.at[1], yrecv.at[0], hsend.at[3], hrecv.at[3], yhi),
    ]
    for copy in halos:
        copy.start()

    names = help_ref[0].astype(jnp.float32)
    sub = lax.broadcasted_iota(jnp.int32, (slots, slots), 0)
    lane = lax.broadcasted_iota(jnp.int32, (slots, slots), 1)
    spread = jnp.broadcast_to(names, (slots, slots))
    column = jnp.sum(jnp.where(sub == lane, spread, 0.0), axis=1, keepdims=True)
    ranks = jnp.sum(jnp.where((column == spread) & (sub < lane), 1.0, 0.0), axis=0, keepdims=True)
    place = names * float(cap) + ranks
    live = lax.broadcasted_iota(jnp.int32, (1, slots), 1) < live_ref[...]
    place = jnp.where(live, place, -1.0)
    cells = cells_ref[0, 0]
    shift = nz.bit_length() - 1
    cell_row = ((cells >> shift) + 1).astype(jnp.float32).astype(jnp.bfloat16)
    cell_z = ((cells & (nz - 1)) + 1).astype(jnp.float32).astype(jnp.bfloat16)
    total = ngy * rows
    target_row = lax.broadcasted_iota(jnp.int32, (total, slots), 0) * pack
    parts_r, parts_z = [], []
    for j in range(pack):
        hot = jnp.where((target_row + j).astype(jnp.float32) == place, 1.0, 0.0).astype(jnp.bfloat16)
        parts_r.append(jnp.dot(hot, cell_row, preferred_element_type=jnp.float32))
        parts_z.append(jnp.dot(hot, cell_z, preferred_element_type=jnp.float32))
    ridx[...] = jnp.concatenate(parts_r, axis=1).astype(jnp.int32) - 1
    zidx[...] = jnp.concatenate(parts_z, axis=1).astype(jnp.int32) - 1

    def lane_row(ref, h):
        return jnp.concatenate([ref[pl.ds(h * rows + i, 1), :] for i in range(rows)], axis=1)

    def one_hots(h, carry):
        r_of = lane_row(ridx, h)
        z_of = lane_row(zidx, h)
        ohr[h] = jnp.where(lax.broadcasted_iota(jnp.int32, (cells_xy, entries), 0) == r_of, 1.0, 0.0).astype(jnp.bfloat16)
        ohz[h] = jnp.where(lax.broadcasted_iota(jnp.int32, (nz, entries), 0) == z_of, 1.0, 0.0).astype(jnp.bfloat16)
        return carry

    lax.fori_loop(0, ngy, one_hots, 0)

    def z_part(x, carry):
        for v, t in enumerate(cyclic_divergence([px[v, x + 2] for v in range(5)], 2, 1)):
            acc[v, x + 1] = t
        return carry

    lax.fori_loop(0, cx, z_part, 0)

    for copy in later:
        copy.wait()

    def weights(t, carry):
        b = t // rows
        i = t % rows
        for part in range(2):
            for j in range(pack):
                high, low = split2(wv[b, i * pack + j])
                piece = high if part == 0 else low
                blank = jnp.zeros((nbr, nbr), jnp.bfloat16)
                full = jnp.concatenate([blank] * j + [piece] + [blank] * (pack - 1 - j), axis=1)
                wbd[t, pl.ds(part * LANES + j * nbr, nbr), :] = full
        return carry

    lax.fori_loop(0, total, weights, 0)

    halos[0].wait_recv()
    halos[1].wait_recv()

    jump0 = [px[v, 1] - px[v, 0] for v in range(5)]
    jump1 = [px[v, 2] - px[v, 1] for v in range(5)]
    low0 = [px[v, 1] + 0.5 * minmod(jump0[v], jump1[v]) for v in range(5)]

    def x_part(f, carry):
        lower, jump, before = carry
        here = [px[v, f + 2] for v in range(5)]
        ahead = [px[v, f + 3] - here[v] for v in range(5)]
        halves = [0.5 * minmod(a, b) for a, b in zip(jump, ahead)]
        flux = double_flux(lower, [t - s for t, s in zip(here, halves)], 0)
        for v in range(5):
            acc[v, f] += flux[v] - before[v]
        return [t + s for t, s in zip(here, halves)], ahead, flux

    for v in range(5):
        acc[v, 0] = jnp.zeros((cy, nz), jnp.float32)
    lax.fori_loop(0, cx + 1, x_part, (low0, jump1, [jnp.zeros((cy, nz), jnp.float32)] * 5))

    halos[2].wait_recv()
    halos[3].wait_recv()

    def y_part(x, carry):
        for v in range(5):
            py[v, x, pl.ds(cy, 2), :] = yrecv[1, v, x]
            py[v, x, pl.ds(cy + 2, 2), :] = yrecv[1, v, x]
            py[v, x, pl.ds(cy + 4, 2), :] = yrecv[0, v, x]
            py[v, x, pl.ds(cy + 6, 2), :] = yrecv[0, v, x]
        q = [py[v, x] for v in range(5)]
        div = cyclic_divergence(q, 1, 0)
        scale = (-2.0 * STEP_RATIO) / (1.0 + cutv[x].astype(jnp.float32))
        cons = conserved([t[0:cy] for t in q])
        for v in range(5):
            delta = (acc[v, x + 1] + div[v][0:cy]) * scale
            out_ref[v, x] = cons[v] + delta
            high, low = split2(delta)
            start = pl.multiple_of(x * cy, cy)
            dmat[v, pl.ds(start, cy), pl.ds(0, nz)] = high
            dmat[v, pl.ds(start, cy), pl.ds(nz, nz)] = low
        return carry

    lax.fori_loop(0, cx, y_part, 0)

    def gather(k, h):
        hot_z = ohz[h]
        stacked = jnp.concatenate([hot_z, hot_z], axis=0)
        mask = lax.broadcasted_iota(jnp.int32, (cells_xy, entries), 0) == lane_row(ridx, h)
        for v in range(5):
            picked = jnp.dot(dmat[v], stacked, preferred_element_type=jnp.float32)
            sendv[k, pl.ds(v, 1), :] = jnp.sum(jnp.where(mask, picked, 0.0), axis=0, keepdims=True)

    def mix(source, k, dest):
        b = lax.rem(gy + ngy - k, ngy)
        for i in range(rows):
            high, low = split2(source[k, :, pl.ds(i * LANES, LANES)])
            w = wbd[b * rows + i]
            first = lax.dot_general(high, w, NT, preferred_element_type=jnp.float32)
            second = lax.dot_general(low, w[0:LANES], NT, preferred_element_type=jnp.float32)
            dest[k, :, pl.ds(i * LANES, LANES)] = first[:, 0:LANES] + first[:, LANES:] + second

    def scatter(k):
        h = lax.rem(gy + k, ngy)
        high, low = split2(returned[k] - sendv[k])
        hot_r = ohr[h]
        hot_z = ohz[h]
        for v in range(5):
            moved = lax.dot_general(hot_r * high[v:v + 1], hot_z, NT, preferred_element_type=jnp.float32)
            moved += lax.dot_general(hot_r * low[v:v + 1], hot_z, NT, preferred_element_type=jnp.float32)
            out_ref[v] += moved.reshape(cx, cy, nz)

    out_copies, back_copies = [None], [None]
    for k in range(1, ngy):
        target = {"gy": lax.rem(gy + k, ngy)}
        gather(k, lax.rem(gy + k, ngy))
        copy = remote(sendv.at[k], arrived.at[k], asend.at[k], arecv.at[k], target)
        copy.start()
        out_copies.append(copy)
    gather(0, gy)
    mix(sendv, 0, returned)
    for k in range(1, ngy):
        out_copies[k].wait_recv()
        mix(arrived, k, mixed)
        source = {"gy": lax.rem(gy + ngy - k, ngy)}
        copy = remote(mixed.at[k], returned.at[k], bsend.at[k], brecv.at[k], source)
        copy.start()
        back_copies.append(copy)
    scatter(0)
    for k in range(1, ngy):
        back_copies[k].wait_recv()
        scatter(k)
    for copy in halos + out_copies[1:] + back_copies[1:]:
        copy.wait_send()


def local(ngx, ngy, dens_pres, velocity, cut_class, nbhd_cells, helper_list, live_counts, redist_weights):
    _, cx, cy, nz = dens_pres.shape
    cap, nbr = redist_weights.shape[3:5]
    pack = LANES // nbr
    rows = cap // pack
    total = ngy * rows
    entries = cap * nbr
    f32, bf16 = jnp.float32, jnp.bfloat16
    hbm = pl.BlockSpec(memory_space=pl.ANY)
    vmem = pl.BlockSpec(memory_space=pltpu.VMEM)
    dma = pltpu.SemaphoreType.DMA
    return pl.pallas_call(
        functools.partial(kernel, ngx, ngy),
        out_shape=jax.ShapeDtypeStruct((5, cx, cy, nz), f32),
        in_specs=[hbm, hbm, hbm, vmem, vmem, vmem, hbm],
        out_specs=vmem,
        scratch_shapes=[
            pltpu.VMEM((5, cx + 4, cy, nz), f32),
            pltpu.VMEM((5, cx, cy + 8, nz), f32),
            pltpu.VMEM((2, 5, cx, 2, nz), f32),
            pltpu.VMEM((2, 5, cx, 2, nz), f32),
            pltpu.VMEM((cx, cy, nz), jnp.int32),
            pltpu.VMEM((ngy, cap, nbr, nbr), f32),
            pltpu.VMEM((5, cx + 1, cy, nz), f32),
            pltpu.VMEM((5, cx * cy, 2 * nz), bf16),
            pltpu.VMEM((total, LANES), jnp.int32),
            pltpu.VMEM((total, LANES), jnp.int32),
            pltpu.VMEM((ngy, cx * cy, entries), bf16),
            pltpu.VMEM((ngy, nz, entries), bf16),
            pltpu.VMEM((total, 2 * LANES, LANES), bf16),
            pltpu.VMEM((ngy, 5, entries), f32),
            pltpu.VMEM((ngy, 5, entries), f32),
            pltpu.VMEM((ngy, 5, entries), f32),
            pltpu.VMEM((ngy, 5, entries), f32),
            dma((5,)), dma((4,)), dma((4,)),
            dma((ngy,)), dma((ngy,)), dma((ngy,)), dma((ngy,)),
        ],
        compiler_params=pltpu.CompilerParams(
            collective_id=0, has_side_effects=True, vmem_limit_bytes=48 * 1024 * 1024
        ),
        name="euler_section",
    )(dens_pres, velocity, cut_class, nbhd_cells, helper_list, live_counts, redist_weights)


def solution(mesh):
    in_specs = (
        P(None, "gx", "gy", None),
        P(None, "gx", "gy", None),
        P("gx", "gy", None),
        P("gx", "gy", None, None),
        P("gx", "gy", None),
        P("gx", "gy"),
        P("gx", "gy", None, None, None, None),
    )
    out_specs = P(None, "gx", "gy", None)
    body = functools.partial(local, mesh.shape["gx"], mesh.shape["gy"])
    return jax.shard_map(body, mesh=mesh, in_specs=in_specs, out_specs=out_specs, check_vma=False)
```

time: 149 us -> 33.4 us (0.22)
  local copies, waits for them, and re-layouts: 94.6 us -> 6.35 us
  Pallas kernels: 0 us -> 26.1 us
  other arithmetic: 21.9 us -> 0 us
  starting transfers between devices: 14.4 us -> 0 us
  waiting for transfers between devices: 11.9 us -> 0 us
  matrix products: 3.94 us -> 0 us
    gather x4 -> x0, local copies, waits for them, and re-layouts: 72.3 us -> none  [the longest x2 59.7 us: local(): fetched = jnp.take(results, jnp.maximum(entry_of, 0), axis=1)]
    pallas_call x0 -> x1, Pallas kernels: none -> 26.1 us  [local(): pl.pallas_call(functools.partial(kernel, ngx, ngy), out_shape=jax.ShapeDt...]
    all_to_all x2 -> x0, waiting for transfers between devices: 11.9 us -> none  [the longest x1 6.23 us: local(): lax.all_to_all(outgoing, 'gy', split_axis=0, concat_axis=0, tiled=True)]
    scatter x1 -> x0, local copies, waits for them, and re-layouts: 8.09 us -> none  [local(): entry_of = jnp.full((total_cells,), -1, jnp.int32).at[cells.reshape(-1)]....]
    ppermute x4 -> x0, starting transfers between devices: 7.73 us -> none  [the longest x2 5 us: padded_2(): lax.ppermute(head, axis, [((i + 1) % count, i) for i in range(count)])]
    all_to_all x2 -> x0, starting transfers between devices: 6.71 us -> none  [the longest x1 3.36 us: local(): lax.all_to_all(outgoing, 'gy', split_axis=0, concat_axis=0, tiled=True)]
    div x1 -> x0, local copies, waits for them, and re-layouts: 4.7 us -> none  [local(): delta = -STEP_RATIO * total_div / kappa[None]]
    sub x9 -> x0, other arithmetic: 4.63 us -> none  [the longest x3 2.31 us: divergence(): piece(centres, 1, length + 2, axis)]
  transfers between devices with their start and end apart: 6 -> 0, of which waited for: 2 -> 0; matrix products, arithmetic and copies ran while one was open for 18% -> 0% of each run, Pallas kernels for 0% -> 0%
where the time goes in v1:
time: 33.4 us; the launch traced here: 33.1 us
  Pallas kernels  26.1 us (78%)
  local copies, waits for them, and re-layouts  6.35 us (19%)
  between operations  0.67 us (2%)
    pallas_call x1, Pallas kernels, local(): pl.pallas_call(functools.partial(kernel, ngx, ngy), out_shape=jax.ShapeDt...  26.1 us
    unnamed x13, local copies, waits for them, and re-layouts  6.35 us

profile of v1, /device:TPU:0, one launch (start us, length us, event | category | flops | bytes accessed | tf_op | source)
XLA Modules:
  0.0 33.1 jit_solution(5057992753218956750)
XLA Ops:
  0.7 0.0 copy-start
  0.7 1.6 %copy-done = f32[1,1,8,8,64,64]{5,4,3,2,1,0:T(8,128)S(1)} copy-done((f32[1,1,8,8,64,64]{5,4,3,2,1,0:T(8,128)S(1)}, f32[1,1,8,8,64,64]{5,4,3,2,1,0:T(8,128)}, u32[]{:S(2)}) %copy-start) | copy-done | bytes 1048600
  2.2 0.0 copy-start.1
  2.2 0.9 %copy-done.1 = f32[3,8,16,128]{3,2,1,0:T(8,128)S(1)} copy-done((f32[3,8,16,128]{3,2,1,0:T(8,128)S(1)}, f32[3,8,16,128]{3,2,1,0:T(8,128)}, u32[]{:S(2)}) %copy-start.1) | copy-done | bytes 196632
  3.2 0.0 copy-start.2
  3.2 0.9 %copy-done.2 = f32[2,8,16,128]{3,2,1,0:T(8,128)S(1)} copy-done((f32[2,8,16,128]{3,2,1,0:T(8,128)S(1)}, f32[2,8,16,128]{3,2,1,0:T(8,128)}, u32[]{:S(2)}) %copy-start.2) | copy-done | bytes 131096
  4.1 0.0 copy-start.3
  4.1 0.8 %copy-done.3 = s32[8,16,128]{2,1,0:T(8,128)S(1)} copy-done((s32[8,16,128]{2,1,0:T(8,128)S(1)}, s32[8,16,128]{2,1,0:T(8,128)}, u32[]{:S(2)}) %copy-start.3) | copy-done | bytes 65560
  4.9 0.0 copy-start.4
  4.9 0.7 %copy-done.4 = s32[1,1,32,64]{3,2,1,0:T(8,128)S(1)} copy-done((s32[1,1,32,64]{3,2,1,0:T(8,128)S(1)}, s32[1,1,32,64]{3,2,1,0:T(8,128)}, u32[]{:S(2)}) %copy-start.4) | copy-done | bytes 8216
  5.6 0.0 copy-start.5
  5.6 0.7 %copy-done.5 = s32[1,1,32]{2,1,0:T(1,128)S(1)} copy-done((s32[1,1,32]{2,1,0:T(1,128)S(1)}, s32[1,1,32]{2,1,0:T(1,128)}, u32[]{:S(2)}) %copy-start.5) | copy-done | bytes 152
  6.3 26.1 %euler_section.1 = f32[5,8,16,128]{3,2,1,0:T(8,128)S(1)} custom-call(f32[2,8,16,128]{3,2,1,0:T(8,128)S(1)} %copy-done.2, f32[3,8,16,128]{3,2,1,0:T(8,128)S(1)} %copy-done.1, s32[8,16,128]{2,1,0:T(8,128)S(1)} %copy-done.3, s32[1,1,32,64]{3,2,1,0:T(8,128)S(1)} %copy-done.4, s32[1,1,32]{2,1,0:T(1,128)S(1)} %copy-done.5, s32[1,1]{1,0:T(1,128)S(6)} %copy.9.live_ref, ...), custom_call_target="tpu_custom_call" | custom-call | tf_op jit(solution)/shard_map/euler_section/pallas_call | solution.py:290
  32.4 0.7 %copy.10 = f32[5,8,16,128]{3,2,1,0:T(8,128)} copy(f32[5,8,16,128]{3,2,1,0:T(8,128)S(1)} %euler_section.1) | data formatting | bytes 655360
Async XLA Ops:
  0.7 1.6 %copy-start = (f32[1,1,8,8,64,64]{5,4,3,2,1,0:T(8,128)S(1)}, f32[1,1,8,8,64,64]{5,4,3,2,1,0:T(8,128)}, u32[]{:S(2)}) copy-start(f32[1,1,8,8,64,64]{5,4,3,2,1,0:T(8,128)} %w_ref.1) | copy-start | bytes 3145732
  2.2 0.9 %copy-start.1 = (f32[3,8,16,128]{3,2,1,0:T(8,128)S(1)}, f32[3,8,16,128]{3,2,1,0:T(8,128)}, u32[]{:S(2)}) copy-start(f32[3,8,16,128]{3,2,1,0:T(8,128)} %vel_ref.1) | copy-start | bytes 589828
  3.2 0.9 %copy-start.2 = (f32[2,8,16,128]{3,2,1,0:T(8,128)S(1)}, f32[2,8,16,128]{3,2,1,0:T(8,128)}, u32[]{:S(2)}) copy-start(f32[2,8,16,128]{3,2,1,0:T(8,128)} %dp_ref.1) | copy-start | bytes 393220
  4.1 0.8 %copy-start.3 = (s32[8,16,128]{2,1,0:T(8,128)S(1)}, s32[8,16,128]{2,1,0:T(8,128)}, u32[]{:S(2)}) copy-start(s32[8,16,128]{2,1,0:T(8,128)} %cut_ref.1) | copy-start | bytes 196612
  4.9 0.7 %copy-start.4 = (s32[1,1,32,64]{3,2,1,0:T(8,128)S(1)}, s32[1,1,32,64]{3,2,1,0:T(8,128)}, u32[]{:S(2)}) copy-start(s32[1,1,32,64]{3,2,1,0:T(8,128)} %cells_ref.1) | copy-start | bytes 24580
  5.6 0.7 %copy-start.5 = (s32[1,1,32]{2,1,0:T(1,128)S(1)}, s32[1,1,32]{2,1,0:T(1,128)}, u32[]{:S(2)}) copy-start(s32[1,1,32]{2,1,0:T(1,128)} %help_ref.1) | copy-start | bytes 388

commit v2 on v1

--- a/solution.py
+++ b/solution.py
@@ -59,7 +59,7 @@
 
 
 def kernel(ngx, ngy, dp_ref, vel_ref, cut_ref, cells_ref, help_ref, live_ref, w_ref, out_ref,
-           px, py, ysend, yrecv, cutv, wv, acc, dmat, ridx, zidx, ohr, ohz, wbd,
+           px, py, ysend, yrecv, cutv, cellv, helpv, livev, wv, acc, dmat, ridx, zidx, ohr, ohz, wbd,
            sendv, arrived, mixed, returned,
            lsem, hsend, hrecv, asend, arecv, bsend, brecv):
     gx = lax.axis_index("gx")
@@ -81,7 +81,12 @@
         pltpu.make_async_copy(w_ref.at[0, 0], wv, lsem.at[3]),
         pltpu.make_async_copy(cut_ref, cutv, lsem.at[4]),
     ]
-    for copy in loads + later:
+    tables = [
+        pltpu.make_async_copy(cells_ref, cellv, lsem.at[5]),
+        pltpu.make_async_copy(help_ref, helpv, lsem.at[6]),
+        pltpu.make_async_copy(live_ref, livev, lsem.at[7]),
+    ]
+    for copy in loads + tables + later:
         copy.start()
 
     xlo = {"gx": lax.rem(gx + ngx - 1, ngx)}
@@ -121,16 +126,18 @@
     for copy in halos:
         copy.start()
 
-    names = help_ref[0].astype(jnp.float32)
+    for copy in tables:
+        copy.wait()
+    names = helpv[0].astype(jnp.float32)
     sub = lax.broadcasted_iota(jnp.int32, (slots, slots), 0)
     lane = lax.broadcasted_iota(jnp.int32, (slots, slots), 1)
     spread = jnp.broadcast_to(names, (slots, slots))
     column = jnp.sum(jnp.where(sub == lane, spread, 0.0), axis=1, keepdims=True)
     ranks = jnp.sum(jnp.where((column == spread) & (sub < lane), 1.0, 0.0), axis=0, keepdims=True)
     place = names * float(cap) + ranks
-    live = lax.broadcasted_iota(jnp.int32, (1, slots), 1) < live_ref[...]
+    live = lax.broadcasted_iota(jnp.int32, (1, slots), 1) < livev[...]
     place = jnp.where(live, place, -1.0)
-    cells = cells_ref[0, 0]
+    cells = cellv[0, 0]
     shift = nz.bit_length() - 1
     cell_row = ((cells >> shift) + 1).astype(jnp.float32).astype(jnp.bfloat16)
     cell_z = ((cells & (nz - 1)) + 1).astype(jnp.float32).astype(jnp.bfloat16)
@@ -148,9 +155,7 @@
         return jnp.concatenate([ref[pl.ds(h * rows + i, 1), :] for i in range(rows)], axis=1)
 
     def one_hots(h, carry):
-        r_of = lane_row(ridx, h)
         z_of = lane_row(zidx, h)
-        ohr[h] = jnp.where(lax.broadcasted_iota(jnp.int32, (cells_xy, entries), 0) == r_of, 1.0, 0.0).astype(jnp.bfloat16)
         ohz[h] = jnp.where(lax.broadcasted_iota(jnp.int32, (nz, entries), 0) == z_of, 1.0, 0.0).astype(jnp.bfloat16)
         return carry
 
@@ -166,6 +171,89 @@
     for copy in later:
         copy.wait()
 
+    halos[0].wait_recv()
+    halos[1].wait_recv()
+
+    jump0 = [px[v, 1] - px[v, 0] for v in range(5)]
+    jump1 = [px[v, 2] - px[v, 1] for v in range(5)]
+    low0 = [px[v, 1] + 0.5 * minmod(jump0[v], jump1[v]) for v in range(5)]
+
+    def x_part(f, carry):
+        lower, jump, before = carry
+        here = [px[v, f + 2] for v in range(5)]
+        ahead = [px[v, f + 3] - here[v] for v in range(5)]
+        halves = [0.5 * minmod(a, b) for a, b in zip(jump, ahead)]
+        flux = double_flux(lower, [t - s for t, s in zip(here, halves)], 0)
+        for v in range(5):
+            acc[v, f] += flux[v] - before[v]
+        return [t + s for t, s in zip(here, halves)], ahead, flux
+
+    for v in range(5):
+        acc[v, 0] = jnp.zeros((cy, nz), jnp.float32)
+    lax.fori_loop(0, cx + 1, x_part, (low0, jump1, [jnp.zeros((cy, nz), jnp.float32)] * 5))
+
+    halos[2].wait_recv()
+    halos[3].wait_recv()
+
+    def y_part(x, carry):
+        for v in range(5):
+            py[v, x, pl.ds(cy, 2), :] = yrecv[1, v, x]
+            py[v, x, pl.ds(cy + 2, 2), :] = yrecv[1, v, x]
+            py[v, x, pl.ds(cy + 4, 2), :] = yrecv[0, v, x]
+            py[v, x, pl.ds(cy + 6, 2), :] = yrecv[0, v, x]
+        q = [py[v, x] for v in range(5)]
+        div = cyclic_divergence(q, 1, 0)
+        scale = (-2.0 * STEP_RATIO) / (1.0 + cutv[x].astype(jnp.float32))
+        cons = conserved([t[0:cy] for t in q])
+        for v in range(5):
+            delta = (acc[v, x + 1] + div[v][0:cy]) * scale
+            out_ref[v, x] = cons[v] + delta
+            high, low = split2(delta)
+            start = pl.multiple_of(x * cy, cy)
+            dmat[v, pl.ds(start, cy), pl.ds(0, nz)] = high
+            dmat[v, pl.ds(start, cy), pl.ds(nz, nz)] = low
+        return carry
+
+    lax.fori_loop(0, cx, y_part, 0)
+
+    def gather(k, h):
+        hot_z = ohz[h]
+        stacked = jnp.concatenate([hot_z, hot_z], axis=0)
+        mask = lax.broadcasted_iota(jnp.int32, (cells_xy, entries), 0) == lane_row(ridx, h)
+        for v in range(5):
+            picked = jnp.dot(dmat[v], stacked, preferred_element_type=jnp.float32)
+            line = jnp.sum(jnp.where(mask, picked, 0.0), axis=0, keepdims=True)
+            for i in range(rows):
+                sendv[k, pl.ds(i * 5 + v, 1), :] = line[:, i * LANES:(i + 1) * LANES]
+
+    def mix(source, k, dest):
+        b = lax.rem(gy + ngy - k, ngy)
+        for i in range(rows):
+            high, low = split2(source[k, pl.ds(i * 5, 5), :])
+            w = wbd[b * rows + i]
+            first = lax.dot_general(high, w, NT, preferred_element_type=jnp.float32)
+            second = lax.dot_general(low, w[0:LANES], NT, preferred_element_type=jnp.float32)
+            dest[k, pl.ds(i * 5, 5), :] = first[:, 0:LANES] + first[:, LANES:] + second
+
+    def scatter(k):
+        h = lax.rem(gy + k, ngy)
+        change = returned[k] - sendv[k]
+        hot_r = ohr[h]
+        hot_z = ohz[h]
+        for v in range(5):
+            line = jnp.concatenate([change[i * 5 + v:i * 5 + v + 1] for i in range(rows)], axis=1)
+            high, low = split2(line)
+            moved = lax.dot_general(hot_r * high, hot_z, NT, preferred_element_type=jnp.float32)
+            moved += lax.dot_general(hot_r * low, hot_z, NT, preferred_element_type=jnp.float32)
+            out_ref[v] += moved.reshape(cx, cy, nz)
+
+    out_copies, back_copies = [None], [None]
+    for k in range(1, ngy):
+        target = {"gy": lax.rem(gy + k, ngy)}
+        gather(k, lax.rem(gy + k, ngy))
+        copy = remote(sendv.at[k], arrived.at[k], asend.at[k], arecv.at[k], target)
+        copy.start()
+        out_copies.append(copy)
     def weights(t, carry):
         b = t // rows
         i = t % rows
@@ -180,85 +268,6 @@
 
     lax.fori_loop(0, total, weights, 0)
 
-    halos[0].wait_recv()
-    halos[1].wait_recv()
-
-    jump0 = [px[v, 1] - px[v, 0] for v in range(5)]
-    jump1 = [px[v, 2] - px[v, 1] for v in range(5)]
-    low0 = [px[v, 1] + 0.5 * minmod(jump0[v], jump1[v]) for v in range(5)]
-
-    def x_part(f, carry):
-        lower, jump, before = carry
-        here = [px[v, f + 2] for v in range(5)]
-        ahead = [px[v, f + 3] - here[v] for v in range(5)]
-        halves = [0.5 * minmod(a, b) for a, b in zip(jump, ahead)]
-        flux = double_flux(lower, [t - s for t, s in zip(here, halves)], 0)
-        for v in range(5):
-            acc[v, f] += flux[v] - before[v]
-        return [t + s for t, s in zip(here, halves)], ahead, flux
-
-    for v in range(5):
-        acc[v, 0] = jnp.zeros((cy, nz), jnp.float32)
-    lax.fori_loop(0, cx + 1, x_part, (low0, jump1, [jnp.zeros((cy, nz), jnp.float32)] * 5))
-
-    halos[2].wait_recv()
-    halos[3].wait_recv()
-
-    def y_part(x, carry):
-        for v in range(5):
-            py[v, x, pl.ds(cy, 2), :] = yrecv[1, v, x]
-            py[v, x, pl.ds(cy + 2, 2), :] = yrecv[1, v, x]
-            py[v, x, pl.ds(cy + 4, 2), :] = yrecv[0, v, x]
-            py[v, x, pl.ds(cy + 6, 2), :] = yrecv[0, v, x]
-        q = [py[v, x] for v in range(5)]
-        div = cyclic_divergence(q, 1, 0)
-        scale = (-2.0 * STEP_RATIO) / (1.0 + cutv[x].astype(jnp.float32))
-        cons = conserved([t[0:cy] for t in q])
-        for v in range(5):
-            delta = (acc[v, x + 1] + div[v][0:cy]) * scale
-            out_ref[v, x] = cons[v] + delta
-            high, low = split2(delta)
-            start = pl.multiple_of(x * cy, cy)
-            dmat[v, pl.ds(start, cy), pl.ds(0, nz)] = high
-            dmat[v, pl.ds(start, cy), pl.ds(nz, nz)] = low
-        return carry
-
-    lax.fori_loop(0, cx, y_part, 0)
-
-    def gather(k, h):
-        hot_z = ohz[h]
-        stacked = jnp.concatenate([hot_z, hot_z], axis=0)
-        mask = lax.broadcasted_iota(jnp.int32, (cells_xy, entries), 0) == lane_row(ridx, h)
-        for v in range(5):
-            picked = jnp.dot(dmat[v], stacked, preferred_element_type=jnp.float32)
-            sendv[k, pl.ds(v, 1), :] = jnp.sum(jnp.where(mask, picked, 0.0), axis=0, keepdims=True)
-
-    def mix(source, k, dest):
-        b = lax.rem(gy + ngy - k, ngy)
-        for i in range(rows):
-            high, low = split2(source[k, :, pl.ds(i * LANES, LANES)])
-            w = wbd[b * rows + i]
-            first = lax.dot_general(high, w, NT, preferred_element_type=jnp.float32)
-            second = lax.dot_general(low, w[0:LANES], NT, preferred_element_type=jnp.float32)
-            dest[k, :, pl.ds(i * LANES, LANES)] = first[:, 0:LANES] + first[:, LANES:] + second
-
-    def scatter(k):
-        h = lax.rem(gy + k, ngy)
-        high, low = split2(returned[k] - sendv[k])
-        hot_r = ohr[h]
-        hot_z = ohz[h]
-        for v in range(5):
-            moved = lax.dot_general(hot_r * high[v:v + 1], hot_z, NT, preferred_element_type=jnp.float32)
-            moved += lax.dot_general(hot_r * low[v:v + 1], hot_z, NT, preferred_element_type=jnp.float32)
-            out_ref[v] += moved.reshape(cx, cy, nz)
-
-    out_copies, back_copies = [None], [None]
-    for k in range(1, ngy):
-        target = {"gy": lax.rem(gy + k, ngy)}
-        gather(k, lax.rem(gy + k, ngy))
-        copy = remote(sendv.at[k], arrived.at[k], asend.at[k], arecv.at[k], target)
-        copy.start()
-        out_copies.append(copy)
     gather(0, gy)
     mix(sendv, 0, returned)
     for k in range(1, ngy):
@@ -268,6 +277,13 @@
         copy = remote(mixed.at[k], returned.at[k], bsend.at[k], brecv.at[k], source)
         copy.start()
         back_copies.append(copy)
+    def row_hots(h, carry):
+        r_of = lane_row(ridx, h)
+        ohr[h] = jnp.where(lax.broadcasted_iota(jnp.int32, (cells_xy, entries), 0) == r_of, 1.0, 0.0).astype(jnp.bfloat16)
+        return carry
+
+    lax.fori_loop(0, ngy, row_hots, 0)
+
     scatter(0)
     for k in range(1, ngy):
         back_copies[k].wait_recv()
@@ -284,13 +300,13 @@
     total = ngy * rows
     entries = cap * nbr
     f32, bf16 = jnp.float32, jnp.bfloat16
-    hbm = pl.BlockSpec(memory_space=pl.ANY)
+    hbm = pl.BlockSpec(memory_space=pltpu.HBM)
     vmem = pl.BlockSpec(memory_space=pltpu.VMEM)
     dma = pltpu.SemaphoreType.DMA
     return pl.pallas_call(
         functools.partial(kernel, ngx, ngy),
         out_shape=jax.ShapeDtypeStruct((5, cx, cy, nz), f32),
-        in_specs=[hbm, hbm, hbm, vmem, vmem, vmem, hbm],
+        in_specs=[hbm] * 7,
         out_specs=vmem,
         scratch_shapes=[
             pltpu.VMEM((5, cx + 4, cy, nz), f32),
@@ -298,6 +314,9 @@
             pltpu.VMEM((2, 5, cx, 2, nz), f32),
             pltpu.VMEM((2, 5, cx, 2, nz), f32),
             pltpu.VMEM((cx, cy, nz), jnp.int32),
+            pltpu.VMEM(nbhd_cells.shape, jnp.int32),
+            pltpu.VMEM(helper_list.shape, jnp.int32),
+            pltpu.VMEM(live_counts.shape, jnp.int32),
             pltpu.VMEM((ngy, cap, nbr, nbr), f32),
             pltpu.VMEM((5, cx + 1, cy, nz), f32),
             pltpu.VMEM((5, cx * cy, 2 * nz), bf16),
@@ -306,15 +325,15 @@
             pltpu.VMEM((ngy, cx * cy, entries), bf16),
             pltpu.VMEM((ngy, nz, entries), bf16),
             pltpu.VMEM((total, 2 * LANES, LANES), bf16),
-            pltpu.VMEM((ngy, 5, entries), f32),
-            pltpu.VMEM((ngy, 5, entries), f32),
-            pltpu.VMEM((ngy, 5, entries), f32),
-            pltpu.VMEM((ngy, 5, entries), f32),
-            dma((5,)), dma((4,)), dma((4,)),
+            pltpu.VMEM((ngy, 5 * rows, LANES), f32),
+            pltpu.VMEM((ngy, 5 * rows, LANES), f32),
+            pltpu.VMEM((ngy, 5 * rows, LANES), f32),
+            pltpu.VMEM((ngy, 5 * rows, LANES), f32),
+            dma((8,)), dma((4,)), dma((4,)),
             dma((ngy,)), dma((ngy,)), dma((ngy,)), dma((ngy,)),
         ],
         compiler_params=pltpu.CompilerParams(
-            collective_id=0, has_side_effects=True, vmem_limit_bytes=48 * 1024 * 1024
+            collective_id=0, has_side_effects=True, vmem_limit_bytes=63 * 1024 * 1024
         ),
         name="euler_section",
     )(dens_pres, velocity, cut_class, nbhd_cells, helper_list, live_counts, redist_weights)

time: 33.4 us -> 27.7 us (0.83)
  local copies, waits for them, and re-layouts: 6.35 us -> 1.72 us
  Pallas kernels: 26.1 us -> 25.1 us
    unnamed x13 -> x1, local copies, waits for them, and re-layouts: 6.35 us -> 1.72 us
    pallas_call x1, Pallas kernels: 26.1 us -> 25.1 us  [local(): pl.pallas_call(functools.partial(kernel, ngx, ngy), out_shape=jax.ShapeDt...]
where the time goes in v2:
time: 27.7 us; the launch traced here: 27.5 us
  Pallas kernels  25.1 us (91%)
  local copies, waits for them, and re-layouts  1.72 us (6%)
  between operations  0.66 us (2%)
    pallas_call x1, Pallas kernels, local(): pl.pallas_call(functools.partial(kernel, ngx, ngy), out_shape=jax.ShapeDt...  25.1 us
    unnamed x1, local copies, waits for them, and re-layouts  1.72 us

profile of v2, /device:TPU:0, one launch (start us, length us, event | category | flops | bytes accessed | tf_op | source)
XLA Modules:
  0.0 27.5 jit_solution(14230289146100178800)
XLA Ops:
  0.7 25.1 %euler_section.1 = f32[5,8,16,128]{3,2,1,0:T(8,128)} custom-call(f32[2,8,16,128]{3,2,1,0:T(8,128)} %dp_ref.1, f32[3,8,16,128]{3,2,1,0:T(8,128)} %vel_ref.1, s32[8,16,128]{2,1,0:T(8,128)} %cut_ref.1, s32[1,1,32,64]{3,2,1,0:T(8,128)} %cells_ref.1, s32[1,1,32]{2,1,0:T(1,128)} %help_ref.1, s32[1,1]{1,0:T(1,128)S(6)} %copy.9.live_ref, f32[1,1,8,8,64,64]{5,4,3,2,1,0:T(8,128)} %w_ref.1), custom_call_target="tpu_custom_call" | custom-call | tf_op jit(solution)/shard_map/euler_section/pallas_call | solution.py:306
  25.8 1.7 %copy.10 = f32[5,8,16,128]{3,2,1,0:T(8,128)} copy(f32[5,8,16,128]{3,2,1,0:T(8,128)} %euler_section.1) | data formatting | bytes 655360
